TPU v7x, 128 devices: a whole 4x4x4 slice. The times are simulated.
128 devices in a mesh: section: 8 (over z, y_lo), expert: 16 (over y_hi, x, core).
Axes of the slice: x: 4, y: 4 (y_hi: 2, y_lo: 2; y = y_hi * 2 + y_lo), z: 4, core: 2. Of those that a mesh axis runs over, the one named last changes fastest.
Arguments:
- act_in: bfloat16 [8, 1024, 3584], P('section', 'expert'), may hold values from -6 to 6
- grad_in: bfloat16 [8, 1024, 3584], P('section', 'expert'), may hold values from -6 to 6
- feed: bfloat16 [1, 1024, 3584], P(None, 'expert'), may hold values from -6 to 6
- loss_grad: bfloat16 [1, 1024, 3584], P(None, 'expert'), may hold values from -6 to 6
- saved: bfloat16 [8, 2, 1024, 3584], P('section', None, 'expert'), may hold values from -6 to 6
- fwd_gain: float32 [8, 3584], P('section'), may hold values from 0.1 to 1.9
- fwd_router: bfloat16 [8, 3584, 8], P('section'), may hold values from -0.09375 to 0.09375
- fwd_gate: bfloat16 [8, 3584, 8192], P('section', None, 'expert'), may hold values from -0.09375 to 0.09375
- fwd_up: bfloat16 [8, 3584, 8192], P('section', None, 'expert'), may hold values from -0.09375 to 0.09375
- fwd_down: bfloat16 [8, 8192, 3584], P('section', 'expert'), may hold values from -0.1875 to 0.1875
- bwd_gain: float32 [8, 3584], P('section'), may hold values from 0.1 to 1.9
- bwd_router: bfloat16 [8, 3584, 8], P('section'), may hold values from -0.09375 to 0.09375
- bwd_gate: bfloat16 [8, 3584, 8192], P('section', None, 'expert'), may hold values from -0.09375 to 0.09375
- bwd_up: bfloat16 [8, 3584, 8192], P('section', None, 'expert'), may hold values from -0.09375 to 0.09375
- bwd_down: bfloat16 [8, 8192, 3584], P('section', 'expert'), may hold values from -0.1875 to 0.1875
- fwd_routes: int32 [8, 2, 1024, 2], P('section', None, 'expert'), may hold values from 0 to 7, as said below
- bwd_routes: int32 [8, 2, 1024, 2], P('section', None, 'expert'), may hold values from 0 to 7, as said below
Outputs:
- fwd_out: bfloat16 [8, 2, 1024, 3584], P('section', None, 'expert')
- bwd_out: bfloat16 [8, 2, 1024, 3584], P('section', None, 'expert')
Inputs may be any that keep to these rules, and one draw needn't show every extreme that they name: `fwd_routes`: each row names 2 different experts. In the 64 rows of one device for one step no expert is named by more than 24 rows; in every step of every layer some expert is named by exactly 24 rows of every device. `bwd_routes`: as for fwd_routes.
All inputs are finite; a program needn't handle non-finite values.
Results may differ from a plain program's by a relative error of at most 0.02.
Values may be sent and summed in bfloat16 or wider, within the bound.
A program may use at most 128 MiB of HBM per device.

v0:
```python
import jax
import jax.numpy as jnp
from jax import lax
from jax.sharding import PartitionSpec as P

SPLIT = 2


NORM_EPS = 1e-06
ROUTE_SCALE = 2.5


def passed_along(value, axis, steps):
    count = lax.axis_size(axis)
    first, last = (max(0, -steps), min(count, count - steps))
    return lax.ppermute(value, axis, [(source, source + steps) for source in range(first, last)])


def to_float(values):
    return values.astype(jnp.float32)


def normalize(inputs, norm_gain):
    widened = to_float(inputs)
    inv_rms = lax.rsqrt(jnp.mean(widened * widened, axis=-1, keepdims=True) + NORM_EPS)
    return ((widened * inv_rms * norm_gain).astype(jnp.bfloat16), inv_rms)


def gating(normed, router, route_ids):
    logits = jnp.dot(normed, router, preferred_element_type=jnp.float32)
    affinity = jax.nn.sigmoid(jnp.take_along_axis(logits, route_ids, axis=1))
    affinity_sum = jnp.sum(affinity, axis=1, keepdims=True)
    return (affinity, affinity_sum, ROUTE_SCALE * affinity / affinity_sum)


def hidden_act(gate_pre, up_pre):
    return (jax.nn.silu(gate_pre) * up_pre).astype(jnp.bfloat16)


def slot_targets(route_ids, experts, capacity):
    flat_ids = route_ids.reshape(-1)
    onehot = (flat_ids[:, None] == jnp.arange(experts, dtype=jnp.int32)[None, :]).astype(jnp.int32)
    earlier = jnp.cumsum(onehot, axis=0) - onehot
    within = jnp.sum(earlier * onehot, axis=1)
    return flat_ids * capacity + within


def pack_slots(values, target, experts, capacity):
    row_count = values.shape[0]
    top_count = target.shape[0] // row_count
    slot_index = jnp.arange(experts * capacity, dtype=jnp.int32)
    chosen = (slot_index[:, None] == target[None, :]).reshape(
        experts * capacity, row_count, top_count
    )
    placer = jnp.any(chosen, axis=2).astype(jnp.bfloat16)
    packed = jnp.dot(placer, values, preferred_element_type=jnp.float32).astype(jnp.bfloat16)
    return packed.reshape(experts, capacity, -1)


def expert_forward(incoming, w_gate, w_up, w_down):
    gate_pre = jnp.einsum("ncd,dh->nch", incoming, w_gate, preferred_element_type=jnp.float32)
    up_pre = jnp.einsum("ncd,dh->nch", incoming, w_up, preferred_element_type=jnp.float32)
    hidden = hidden_act(gate_pre, up_pre)
    return jnp.einsum("nch,hd->ncd", hidden, w_down, preferred_element_type=jnp.float32)


def expert_backward(incoming, w_gate, w_up, w_down):
    normed_rows = incoming[:, :, 0]
    cotangent_rows = incoming[:, :, 1]
    gate_pre = jnp.einsum("ncd,dh->nch", normed_rows, w_gate, preferred_element_type=jnp.float32)
    up_pre = jnp.einsum("ncd,dh->nch", normed_rows, w_up, preferred_element_type=jnp.float32)
    gate_sig = jax.nn.sigmoid(gate_pre)
    hidden = hidden_act(gate_pre, up_pre)
    hidden_grad = jnp.einsum(
        "ncd,hd->nch", cotangent_rows, w_down, preferred_element_type=jnp.float32
    )
    sensitivity = jnp.sum(to_float(hidden) * hidden_grad, axis=-1)
    gate_grad = (hidden_grad * up_pre * gate_sig * (1.0 + gate_pre * (1.0 - gate_sig))).astype(
        jnp.bfloat16
    )
    up_grad = (hidden_grad * jax.nn.silu(gate_pre)).astype(jnp.bfloat16)
    partial_value = jnp.einsum("nch,dh->ncd", gate_grad, w_gate, preferred_element_type=jnp.float32)
    partial_value = partial_value + jnp.einsum(
        "nch,dh->ncd", up_grad, w_up, preferred_element_type=jnp.float32
    )
    return (partial_value, sensitivity)


def forward_group(inputs, norm_gain, router, w_gate, w_up, w_down, route_ids):
    row_count = inputs.shape[0]
    top_count = route_ids.shape[1]
    experts = router.shape[1]
    capacity = row_count * top_count // experts + row_count // 8
    normed, inv_rms = normalize(inputs, norm_gain)
    affinity, affinity_sum, gates = gating(normed, router, route_ids)
    target = slot_targets(route_ids, experts, capacity)
    packed = pack_slots(normed, target, experts, capacity)
    outgoing = jnp.repeat(packed, SPLIT, axis=0)
    partial_value = expert_forward(
        lax.all_to_all(outgoing, "expert", split_axis=0, concat_axis=0, tiled=True),
        w_gate,
        w_up,
        w_down,
    )
    returned = lax.all_to_all(
        partial_value.astype(jnp.bfloat16), "expert", split_axis=0, concat_axis=0, tiled=True
    ).astype(partial_value.dtype)
    expert_out = jnp.sum(returned.reshape(experts, SPLIT, capacity, -1), axis=1).astype(
        jnp.bfloat16
    )
    slot_values = jnp.take(expert_out.reshape(experts * capacity, -1), target, axis=0).reshape(
        row_count, top_count, -1
    )
    result = to_float(inputs) + jnp.sum(gates[:, :, None] * to_float(slot_values), axis=1)
    return result.astype(jnp.bfloat16)


def backward_group(inputs, cotangent, norm_gain, router, w_gate, w_up, w_down, route_ids):
    row_count = inputs.shape[0]
    top_count = route_ids.shape[1]
    experts = router.shape[1]
    width = inputs.shape[1]
    capacity = row_count * top_count // experts + row_count // 8
    normed, inv_rms = normalize(inputs, norm_gain)
    affinity, affinity_sum, gates = gating(normed, router, route_ids)
    target = slot_targets(route_ids, experts, capacity)
    joined = jnp.concatenate([normed, cotangent], axis=1)
    packed = pack_slots(joined, target, experts, capacity).reshape(experts, capacity, 2, width)
    outgoing = jnp.repeat(packed, SPLIT, axis=0)
    partial_value, sensitivity = expert_backward(
        lax.all_to_all(outgoing, "expert", split_axis=0, concat_axis=0, tiled=True),
        w_gate,
        w_up,
        w_down,
    )
    parts_back = lax.all_to_all(
        partial_value.astype(jnp.bfloat16), "expert", split_axis=0, concat_axis=0, tiled=True
    ).astype(partial_value.dtype)
    sens_back = lax.all_to_all(
        sensitivity.astype(jnp.bfloat16), "expert", split_axis=0, concat_axis=0, tiled=True
    ).astype(sensitivity.dtype)
    summed_parts = jnp.sum(parts_back.reshape(experts, SPLIT, capacity, width), axis=1)
    summed_sens = jnp.sum(sens_back.reshape(experts, SPLIT, capacity), axis=1)
    grads_flat = summed_parts.reshape(experts * capacity, width).astype(jnp.bfloat16)
    part_slots = to_float(jnp.take(grads_flat, target, axis=0)).reshape(row_count, top_count, width)
    sens_slots = jnp.take(summed_sens.reshape(-1), target).reshape(row_count, top_count)
    weighted = jnp.sum(affinity * sens_slots, axis=1, keepdims=True)
    logit_grad = (
        ROUTE_SCALE
        / affinity_sum
        * (sens_slots - weighted / affinity_sum)
        * affinity
        * (1.0 - affinity)
    )
    onehot = (route_ids[:, :, None] == jnp.arange(experts, dtype=jnp.int32)[None, None, :]).astype(
        jnp.float32
    )
    spread = jnp.sum(logit_grad[:, :, None] * onehot, axis=1)
    normed_grad = jnp.sum(gates[:, :, None] * part_slots, axis=1)
    normed_grad = normed_grad + jnp.einsum(
        "re,de->rd", spread, to_float(router), precision=lax.Precision.HIGHEST
    )
    widened = to_float(inputs)
    scaled = norm_gain * normed_grad
    inner_sum = jnp.sum(widened * scaled, axis=-1, keepdims=True) / width
    result = to_float(cotangent) + inv_rms * scaled - widened * inv_rms**3 * inner_sum
    return result.astype(jnp.bfloat16)


def per_device(
    act_in,
    grad_in,
    feed,
    loss_grad,
    saved,
    fwd_gain,
    fwd_router,
    fwd_gate,
    fwd_up,
    fwd_down,
    bwd_gain,
    bwd_router,
    bwd_gate,
    bwd_up,
    bwd_down,
    fwd_routes,
    bwd_routes,
):
    tick_count = saved.shape[1]
    first_section = lax.axis_index("section") == 0
    forward_now = act_in[0]
    backward_now = grad_in[0]
    forward_list = []
    backward_list = []
    for step_index in range(tick_count):
        forward_done = forward_group(
            forward_now,
            fwd_gain[0],
            fwd_router[0],
            fwd_gate[0],
            fwd_up[0],
            fwd_down[0],
            fwd_routes[0, step_index],
        )
        backward_done = backward_group(
            saved[0, step_index],
            backward_now,
            bwd_gain[0],
            bwd_router[0],
            bwd_gate[0],
            bwd_up[0],
            bwd_down[0],
            bwd_routes[0, step_index],
        )
        forward_list.append(forward_done)
        backward_list.append(backward_done)
        if step_index + 1 < tick_count:
            moved_forward, moved_backward = passed_along(
                (forward_done, backward_done), "section", 1
            )
            forward_now = jnp.where(first_section, feed[step_index], moved_forward)
            backward_now = jnp.where(first_section, loss_grad[step_index], moved_backward)
    return (jnp.stack(forward_list)[None], jnp.stack(backward_list)[None])


def solution(mesh):
    in_specs = (
        P("section", "expert", None),
        P("section", "expert", None),
        P(None, "expert", None),
        P(None, "expert", None),
        P("section", None, "expert", None),
        P("section", None),
        P("section", None, None),
        P("section", None, "expert"),
        P("section", None, "expert"),
        P("section", "expert", None),
        P("section", None),
        P("section", None, None),
        P("section", None, "expert"),
        P("section", None, "expert"),
        P("section", "expert", None),
        P("section", None, "expert", None),
        P("section", None, "expert", None),
    )
    out_specs = (P("section", None, "expert", None), P("section", None, "expert", None))
    return jax.shard_map(
        per_device, mesh=mesh, in_specs=in_specs, out_specs=out_specs, check_vma=False
    )
```

profile of v0, /device:TPU:96, one launch (start us, length us, event | category | flops | bytes accessed | tf_op | source)
XLA Modules:
  0.0 538.1 jit_solution(10208967350367246247)
XLA Ops:
  9.4 7.2 %all-to-all-start = ((bf16[16,24,3584]{2,1,0:T(8,128)(2,1)}), bf16[16,24,3584]{2,1,0:T(8,128)(2,1)}, u32[]{:S(2)}, u32[]{:S(2)}) async-start(bf16[16,24,3584]{2,1,0:T(8,128)(2,1)} %bitcast.296), calls=%async_computation | async-start | bytes 5505024 | tf_op jit(solution)/shard_map/all_to_all | solution.py:100
  21.5 7.4 %reshape_reshape.6 = bf16[8,24,2,3584]{3,2,1,0:T(2,128)(2,1)} reshape(bf16[192,7168]{1,0:T(8,128)(2,1)} %convolution_convert_fusion.1) | data formatting | bytes 5505024 | tf_op jit(solution)/shard_map/reshape;reshape | solution.py:128
  28.9 3.7 copy.180
  32.5 21.0 %all-to-all-done = bf16[16,24,3584]{2,1,0:T(8,128)(2,1)} async-done(((bf16[16,24,3584]{2,1,0:T(8,128)(2,1)}), bf16[16,24,3584]{2,1,0:T(8,128)(2,1)}, u32[]{:S(2)}, u32[]{:S(2)}) %all-to-all-start) | async-done | bytes 2752544 | tf_op jit(solution)/shard_map/all_to_all | solution.py:100
  53.6 4.8 broadcast_in_dim.33
  58.4 6.2 %all-to-all-start.4 = ((bf16[16,24,2,3584]{3,1,2,0:T(8,128)(2,1)}), bf16[16,24,2,3584]{3,1,2,0:T(8,128)(2,1)}, u32[]{:S(2)}, u32[]{:S(2)}) async-start(bf16[16,24,2,3584]{3,1,2,0:T(8,128)(2,1)} %bitcast.295), calls=%async_computation.4 | async-start | bytes 11010048 | tf_op jit(solution)/shard_map/all_to_all | solution.py:131
  67.1 4.5 fusion.30
  71.6 8.7 %convolution_convert_fusion.3 = bf16[16,24,3584]{2,1,0:T(8,128)(2,1)} fusion(bf16[1,512,3584]{2,1,0:T(8,128)(2,1)} %param.32, bf16[16,24,3584]{2,1,0:T(8,128)(2,1)} %all-to-all-done, bf16[1,3584,512]{2,1,0:T(8,128)(2,1)} %param.31, f32[16,24,512]{2,1,0:T(8,128)S(1)} %fusion.30), kind=kOutput, calls=%fused_computation.17 | convolution fusion | flops 2821128192 | bytes 13631488 | tf_op jit(solution)/shard_map/nch,hd->ncd/dot_general | solution.py:64
  80.2 58.6 %all-to-all-done.4 = bf16[16,24,2,3584]{3,1,2,0:T(8,128)(2,1)} async-done(((bf16[16,24,2,3584]{3,1,2,0:T(8,128)(2,1)}), bf16[16,24,2,3584]{3,1,2,0:T(8,128)(2,1)}, u32[]{:S(2)}, u32[]{:S(2)}) %all-to-all-start.4) | async-done | bytes 5505056 | tf_op jit(solution)/shard_map/all_to_all | solution.py:131
  138.8 6.3 %all-to-all-start.1 = ((bf16[16,24,3584]{2,1,0:T(8,128)(2,1)}), bf16[16,24,3584]{2,1,0:T(8,128)(2,1)}, u32[]{:S(2)}, u32[]{:S(2)}) async-start(bf16[16,24,3584]{2,1,0:T(8,128)(2,1)} %convolution_convert_fusion.3), calls=%async_computation.1 | async-start | bytes 5505024 | tf_op jit(solution)/shard_map/all_to_all | solution.py:105
  145.1 4.6 fusion.10
  149.7 3.6 fusion.16
  153.3 3.8 multiply_reduce_fusion.5
  159.6 3.3 fusion
  162.8 19.2 %all-to-all-done.1 = bf16[16,24,3584]{2,1,0:T(8,128)(2,1)} async-done(((bf16[16,24,3584]{2,1,0:T(8,128)(2,1)}), bf16[16,24,3584]{2,1,0:T(8,128)(2,1)}, u32[]{:S(2)}, u32[]{:S(2)}) %all-to-all-start.1) | async-done | bytes 2752544 | tf_op jit(solution)/shard_map/all_to_all | solution.py:105
  182.0 6.0 %all-to-all-start.6 = ((bf16[16,1,24]{2,1,0:T(2,128)(2,1)}), bf16[16,1,24]{2,1,0:T(2,128)(2,1)S(1)}, u32[]{:S(2)}, u32[]{:S(2)}) async-start(bf16[16,1,24]{2,1,0:T(2,128)(2,1)} %copy.183), calls=%async_computation.6 | async-start | bytes 16384 | tf_op jit(solution)/shard_map/all_to_all | solution.py:139
  191.5 4.1 all-to-all-done.6
  195.5 4.5 all-to-all-start.5
  201.5 3.4 reshape.367
  204.9 4.1 multiply_reduce_fusion.3
  209.0 2.8 collective-permute-start
  215.0 26.2 %collective-permute-done = bf16[64,3584]{1,0:T(8,128)(2,1)} collective-permute-done((bf16[64,3584]{1,0:T(8,128)(2,1)S(1)}, bf16[64,3584]{1,0:T(8,128)(2,1)}, u32[]{:S(2)}, u32[]{:S(2)}) %collective-permute-start) | collective-permute-done | bytes 458784 | tf_op jit(solution)/shard_map/ppermute | solution.py:16
  245.7 7.7 %all-to-all-start.2 = ((bf16[16,24,3584]{2,1,0:T(8,128)(2,1)}), bf16[16,24,3584]{2,1,0:T(8,128)(2,1)}, u32[]{:S(2)}, u32[]{:S(2)}) async-start(bf16[16,24,3584]{2,1,0:T(8,128)(2,1)} %bitcast.297), calls=%async_computation.2 | async-start | bytes 5505024 | tf_op jit(solution)/shard_map/all_to_all | solution.py:100
  260.4 3.3 reshape.371
  263.7 4.1 multiply_reduce_fusion.1
  268.7 21.6 %all-to-all-done.2 = bf16[16,24,3584]{2,1,0:T(8,128)(2,1)} async-done(((bf16[16,24,3584]{2,1,0:T(8,128)(2,1)}), bf16[16,24,3584]{2,1,0:T(8,128)(2,1)}, u32[]{:S(2)}, u32[]{:S(2)}) %all-to-all-start.2) | async-done | bytes 2752544 | tf_op jit(solution)/shard_map/all_to_all | solution.py:100
  290.3 5.4 fusion.28
  295.7 8.9 %convolution_convert_fusion.2 = bf16[16,24,3584]{2,1,0:T(8,128)(2,1)} fusion(bf16[1,512,3584]{2,1,0:T(8,128)(2,1)} %param.32, bf16[16,24,3584]{2,1,0:T(8,128)(2,1)} %all-to-all-done.2, bf16[1,3584,512]{2,1,0:T(8,128)(2,1)} %param.31, f32[16,24,512]{2,1,0:T(8,128)} %fusion.28), kind=kOutput, calls=%fused_computation.16 | convolution fusion | flops 2821128192 | bytes 13631488 | tf_op jit(solution)/shard_map/nch,hd->ncd/dot_general | solution.py:64
  304.6 6.2 %all-to-all-start.3 = ((bf16[16,24,3584]{2,1,0:T(8,128)(2,1)}), bf16[16,24,3584]{2,1,0:T(8,128)(2,1)}, u32[]{:S(2)}, u32[]{:S(2)}) async-start(bf16[16,24,3584]{2,1,0:T(8,128)(2,1)} %convolution_convert_fusion.2), calls=%async_computation.3 | async-start | bytes 5505024 | tf_op jit(solution)/shard_map/all_to_all | solution.py:105
  311.3 2.6 collective-permute-start.1
  314.0 37.7 %collective-permute-done.1 = bf16[64,3584]{1,0:T(8,128)(2,1)S(1)} collective-permute-done((bf16[64,3584]{1,0:T(8,128)(2,1)S(1)}, bf16[64,3584]{1,0:T(8,128)(2,1)S(1)}, u32[]{:S(2)}, u32[]{:S(2)}) %collective-permute-start.1) | collective-permute-done | bytes 458784 | tf_op jit(solution)/shard_map/ppermute | solution.py:16
  355.0 7.4 %reshape_reshape.7 = bf16[8,24,2,3584]{3,2,1,0:T(2,128)(2,1)} reshape(bf16[192,7168]{1,0:T(8,128)(2,1)} %convolution_convert_fusion) | data formatting | bytes 5505024 | tf_op jit(solution)/shard_map/reshape;reshape | solution.py:128
  362.4 3.6 copy.191
  366.0 4.8 broadcast_in_dim.34
  370.8 7.7 %all-to-all-start.7 = ((bf16[16,24,2,3584]{3,1,2,0:T(8,128)(2,1)}), bf16[16,24,2,3584]{3,1,2,0:T(8,128)(2,1)}, u32[]{:S(2)}, u32[]{:S(2)}) async-start(bf16[16,24,2,3584]{3,1,2,0:T(8,128)(2,1)} %bitcast.294), calls=%async_computation.7 | async-start | bytes 11010048 | tf_op jit(solution)/shard_map/all_to_all | solution.py:131
  387.9 3.3 reshape.368
  391.2 61.5 %all-to-all-done.7 = bf16[16,24,2,3584]{3,1,2,0:T(8,128)(2,1)} async-done(((bf16[16,24,2,3584]{3,1,2,0:T(8,128)(2,1)}), bf16[16,24,2,3584]{3,1,2,0:T(8,128)(2,1)}, u32[]{:S(2)}, u32[]{:S(2)}) %all-to-all-start.7) | async-done | bytes 5505056 | tf_op jit(solution)/shard_map/all_to_all | solution.py:131
  452.7 4.6 fusion.13
  457.4 3.7 fusion.6
  461.1 3.6 multiply_reduce_fusion.4
  465.3 6.2 %all-to-all-start.9 = ((bf16[16,1,24]{2,1,0:T(2,128)(2,1)}), bf16[16,1,24]{2,1,0:T(2,128)(2,1)S(1)}, u32[]{:S(2)}, u32[]{:S(2)}) async-start(bf16[16,1,24]{2,1,0:T(2,128)(2,1)} %copy.194), calls=%async_computation.9 | async-start | bytes 16384 | tf_op jit(solution)/shard_map/all_to_all | solution.py:139
  471.6 4.3 fusion.4
  475.9 3.3 fusion.1
  479.1 7.4 %all-to-all-start.8 = ((bf16[16,24,3584]{2,1,0:T(8,128)(2,1)}), bf16[16,24,3584]{2,1,0:T(8,128)(2,1)}, u32[]{:S(2)}, u32[]{:S(2)}) async-start(bf16[16,24,3584]{2,1,0:T(8,128)(2,1)} %fusion.1), calls=%async_computation.8 | async-start | bytes 5505024 | tf_op jit(solution)/shard_map/all_to_all | solution.py:136
  488.4 4.1 multiply_reduce_fusion.2
  493.6 29.8 %all-to-all-done.8 = bf16[16,24,3584]{2,1,0:T(8,128)(2,1)} async-done(((bf16[16,24,3584]{2,1,0:T(8,128)(2,1)}), bf16[16,24,3584]{2,1,0:T(8,128)(2,1)}, u32[]{:S(2)}, u32[]{:S(2)}) %all-to-all-start.8) | async-done | bytes 2752544 | tf_op jit(solution)/shard_map/all_to_all | solution.py:136
  528.3 3.3 reshape.375
  531.6 4.1 multiply_reduce_fusion
  (201 shorter events, 62.3 us)
Async XLA Ops:
  0.6 66.1 %copy-start = (bf16[1,3584,8]{1,2,0:T(8,128)(2,1)S(1)}, bf16[1,3584,8]{1,2,0:T(8,128)(2,1)}, u32[]{:S(2)}) copy-start(bf16[1,3584,8]{1,2,0:T(8,128)(2,1)} %param.34) | copy-start | bytes 172036
  9.4 7.2 %copy-start.22 = (s32[1,2,64,2]{2,3,1,0:T(2,128)S(1)}, s32[1,2,64,2]{2,3,1,0:T(2,128)}, u32[]{:S(2)}) copy-start(s32[1,2,64,2]{2,3,1,0:T(2,128)} %param.39) | copy-start | bytes 3076
  9.4 9.1 %copy-start.24 = (f32[1,3584]{1,0:T(1,128)S(1)}, f32[1,3584]{1,0:T(1,128)}, u32[]{:S(2)}) copy-start(f32[1,3584]{1,0:T(1,128)} %param.33) | copy-start | bytes 43012
  9.4 9.2 %copy-start.5 = (bf16[1,2,64,3584]{3,2,1,0:T(8,128)(2,1)S(1)}, bf16[1,2,64,3584]{3,2,1,0:T(8,128)(2,1)}, u32[]{:S(2)}) copy-start(bf16[1,2,64,3584]{3,2,1,0:T(8,128)(2,1)} %param.27) | copy-start | bytes 2752516
  9.4 9.7 %copy-start.15 = (bf16[1,64,3584]{2,1,0:T(8,128)(2,1)S(1)}, bf16[1,64,3584]{2,1,0:T(8,128)(2,1)}, u32[]{:S(2)}) copy-start(bf16[1,64,3584]{2,1,0:T(8,128)(2,1)} %param.24) | copy-start | bytes 1376260
  9.4 44.2 %all-to-all-start = ((bf16[16,24,3584]{2,1,0:T(8,128)(2,1)}), bf16[16,24,3584]{2,1,0:T(8,128)(2,1)}, u32[]{:S(2)}, u32[]{:S(2)}) async-start(bf16[16,24,3584]{2,1,0:T(8,128)(2,1)} %bitcast.296), calls=%async_computation | async-start | bytes 5505024 | tf_op jit(solution)/shard_map/all_to_all | solution.py:100
  58.4 6.2 %copy-start.23 = (s32[1,2,64,2]{2,3,1,0:T(2,128)S(1)}, s32[1,2,64,2]{2,3,1,0:T(2,128)}, u32[]{:S(2)}) copy-start(s32[1,2,64,2]{2,3,1,0:T(2,128)} %param.38) | copy-start | bytes 3076
  58.4 6.5 %copy-start.6 = (bf16[1,64,3584]{2,1,0:T(8,128)(2,1)S(1)}, bf16[1,64,3584]{2,1,0:T(8,128)(2,1)}, u32[]{:S(2)}) copy-start(bf16[1,64,3584]{2,1,0:T(8,128)(2,1)} %param.23) | copy-start | bytes 1376260
  58.4 6.5 %copy-start.27 = (bf16[1,3584,8]{1,2,0:T(8,128)(2,1)S(1)}, bf16[1,3584,8]{1,2,0:T(8,128)(2,1)}, u32[]{:S(2)}) copy-start(bf16[1,3584,8]{1,2,0:T(8,128)(2,1)} %param.29) | copy-start | bytes 172036
  58.4 80.4 %all-to-all-start.4 = ((bf16[16,24,2,3584]{3,1,2,0:T(8,128)(2,1)}), bf16[16,24,2,3584]{3,1,2,0:T(8,128)(2,1)}, u32[]{:S(2)}, u32[]{:S(2)}) async-start(bf16[16,24,2,3584]{3,1,2,0:T(8,128)(2,1)} %bitcast.295), calls=%async_computation.4 | async-start | bytes 11010048 | tf_op jit(solution)/shard_map/all_to_all | solution.py:131
  138.8 43.2 %all-to-all-start.1 = ((bf16[16,24,3584]{2,1,0:T(8,128)(2,1)}), bf16[16,24,3584]{2,1,0:T(8,128)(2,1)}, u32[]{:S(2)}, u32[]{:S(2)}) async-start(bf16[16,24,3584]{2,1,0:T(8,128)(2,1)} %convolution_convert_fusion.3), calls=%async_computation.1 | async-start | bytes 5505024 | tf_op jit(solution)/shard_map/all_to_all | solution.py:105
  145.1 4.7 copy-start.3
  149.7 3.6 copy-start.25
  153.3 4.4 copy-start.1
  182.0 13.5 %all-to-all-start.6 = ((bf16[16,1,24]{2,1,0:T(2,128)(2,1)}), bf16[16,1,24]{2,1,0:T(2,128)(2,1)S(1)}, u32[]{:S(2)}, u32[]{:S(2)}) async-start(bf16[16,1,24]{2,1,0:T(2,128)(2,1)} %copy.183), calls=%async_computation.6 | async-start | bytes 16384 | tf_op jit(solution)/shard_map/all_to_all | solution.py:139
  195.5 48.4 %all-to-all-start.5 = ((bf16[16,24,3584]{2,1,0:T(8,128)(2,1)}), bf16[16,24,3584]{2,1,0:T(8,128)(2,1)}, u32[]{:S(2)}, u32[]{:S(2)}) async-start(bf16[16,24,3584]{2,1,0:T(8,128)(2,1)} %fusion), calls=%async_computation.5 | async-start | bytes 5505024 | tf_op jit(solution)/shard_map/all_to_all | solution.py:136
  201.5 7.4 %copy-start.7 = (bf16[1,64,3584]{2,1,0:T(8,128)(2,1)S(1)}, bf16[1,64,3584]{2,1,0:T(8,128)(2,1)}, u32[]{:S(2)}) copy-start(bf16[1,64,3584]{2,1,0:T(8,128)(2,1)} %param.23) | copy-start | bytes 1376260
  209.0 32.2 %collective-permute-start = (bf16[64,3584]{1,0:T(8,128)(2,1)S(1)}, bf16[64,3584]{1,0:T(8,128)(2,1)}, u32[]{:S(2)}, u32[]{:S(2)}) collective-permute-start(bf16[64,3584]{1,0:T(8,128)(2,1)S(1)} %fusion.76), channel_id=1, source_target_pairs={{0,16},{16,32},{32,48},{48,64},{64,80},{80,96},{96,112},{1,17},{17... | collective-permute-start | bytes 1376264 | tf_op jit(solution)/shard_map/ppermute | solution.py:16
  212.1 29.2 %copy-start.20 = (bf16[1,64,3584]{2,1,0:T(8,128)(2,1)S(1)}, bf16[1,64,3584]{2,1,0:T(8,128)(2,1)}, u32[]{:S(2)}) copy-start(bf16[1,64,3584]{2,1,0:T(8,128)(2,1)} %param.25) | copy-start | bytes 1376260
  242.6 0.8 copy-start.11
  245.7 44.7 %all-to-all-start.2 = ((bf16[16,24,3584]{2,1,0:T(8,128)(2,1)}), bf16[16,24,3584]{2,1,0:T(8,128)(2,1)}, u32[]{:S(2)}, u32[]{:S(2)}) async-start(bf16[16,24,3584]{2,1,0:T(8,128)(2,1)} %bitcast.297), calls=%async_computation.2 | async-start | bytes 5505024 | tf_op jit(solution)/shard_map/all_to_all | solution.py:100
  304.6 6.2 %copy-start.16 = (bf16[1,64,3584]{2,1,0:T(8,128)(2,1)S(1)}, bf16[1,64,3584]{2,1,0:T(8,128)(2,1)}, u32[]{:S(2)}) copy-start(bf16[1,64,3584]{2,1,0:T(8,128)(2,1)} %param.24) | copy-start | bytes 1376260
  304.6 61.4 %all-to-all-start.3 = ((bf16[16,24,3584]{2,1,0:T(8,128)(2,1)}), bf16[16,24,3584]{2,1,0:T(8,128)(2,1)}, u32[]{:S(2)}, u32[]{:S(2)}) async-start(bf16[16,24,3584]{2,1,0:T(8,128)(2,1)} %convolution_convert_fusion.2), calls=%async_computation.3 | async-start | bytes 5505024 | tf_op jit(solution)/shard_map/all_to_all | solution.py:105
  310.8 40.9 %copy-start.21 = (bf16[1,64,3584]{2,1,0:T(8,128)(2,1)S(1)}, bf16[1,64,3584]{2,1,0:T(8,128)(2,1)}, u32[]{:S(2)}) copy-start(bf16[1,64,3584]{2,1,0:T(8,128)(2,1)} %param.26) | copy-start | bytes 1376260
  311.3 2.7 copy-start.17
  311.3 40.4 %collective-permute-start.1 = (bf16[64,3584]{1,0:T(8,128)(2,1)S(1)}, bf16[64,3584]{1,0:T(8,128)(2,1)S(1)}, u32[]{:S(2)}, u32[]{:S(2)}) collective-permute-start(bf16[64,3584]{1,0:T(8,128)(2,1)S(1)} %get-tuple-element.28), channel_id=1, source_target_pairs={{0,16},{16,32},{32,48},{48,64},{64,80},{80,96},{96,112},{1,17},{17... | collective-permute-start | bytes 1376264 | tf_op jit(solution)/shard_map/ppermute | solution.py:16
  351.8 0.8 copy-start.9
  370.8 8.3 %copy-start.8 = (bf16[1,64,3584]{2,1,0:T(8,128)(2,1)S(1)}, bf16[1,64,3584]{2,1,0:T(8,128)(2,1)}, u32[]{:S(2)}) copy-start(bf16[1,64,3584]{2,1,0:T(8,128)(2,1)} %param.23) | copy-start | bytes 1376260
  370.8 9.2 %copy-start.12 = (bf16[64,3584]{1,0:T(8,128)(2,1)S(1)}, bf16[64,3584]{1,0:T(8,128)(2,1)}, u32[]{:S(2)}) copy-start(bf16[64,3584]{1,0:T(8,128)(2,1)} %copy-done.11) | copy-start | bytes 1376260
  370.8 81.9 %all-to-all-start.7 = ((bf16[16,24,2,3584]{3,1,2,0:T(8,128)(2,1)}), bf16[16,24,2,3584]{3,1,2,0:T(8,128)(2,1)}, u32[]{:S(2)}, u32[]{:S(2)}) async-start(bf16[16,24,2,3584]{3,1,2,0:T(8,128)(2,1)} %bitcast.294), calls=%async_computation.7 | async-start | bytes 11010048 | tf_op jit(solution)/shard_map/all_to_all | solution.py:131
  452.7 4.6 copy-start.2
  457.3 3.7 copy-start.19
  457.4 3.7 copy-start.26
  465.3 13.8 %all-to-all-start.9 = ((bf16[16,1,24]{2,1,0:T(2,128)(2,1)}), bf16[16,1,24]{2,1,0:T(2,128)(2,1)S(1)}, u32[]{:S(2)}, u32[]{:S(2)}) async-start(bf16[16,1,24]{2,1,0:T(2,128)(2,1)} %copy.194), calls=%async_computation.9 | async-start | bytes 16384 | tf_op jit(solution)/shard_map/all_to_all | solution.py:139
  471.5 4.3 copy-start.4
  479.1 44.3 %all-to-all-start.8 = ((bf16[16,24,3584]{2,1,0:T(8,128)(2,1)}), bf16[16,24,3584]{2,1,0:T(8,128)(2,1)}, u32[]{:S(2)}, u32[]{:S(2)}) async-start(bf16[16,24,3584]{2,1,0:T(8,128)(2,1)} %fusion.1), calls=%async_computation.8 | async-start | bytes 5505024 | tf_op jit(solution)/shard_map/all_to_all | solution.py:136
  486.5 6.0 %copy-start.13 = (bf16[64,3584]{1,0:T(8,128)(2,1)S(1)}, bf16[64,3584]{1,0:T(8,128)(2,1)}, u32[]{:S(2)}) copy-start(bf16[64,3584]{1,0:T(8,128)(2,1)} %copy-done.11) | copy-start | bytes 1376260
  486.5 6.1 %copy-start.14 = (bf16[1,64,3584]{2,1,0:T(8,128)(2,1)S(1)}, bf16[1,64,3584]{2,1,0:T(8,128)(2,1)}, u32[]{:S(2)}) copy-start(bf16[1,64,3584]{2,1,0:T(8,128)(2,1)} %fusion.79) | copy-start | bytes 1376260
  531.6 4.9 copy-start.10
  535.7 1.2 copy-start.18
where the time goes:
time: 549 us; the launch traced here: 538 us
  waiting for transfers between devices  280 us (51%)
  matrix products  74 us (13%)
  starting transfers between devices  70.8 us (13%)
  local copies, waits for them, and re-layouts  68.4 us (12%)
  other arithmetic  43.2 us (8%)
    all_to_all x2, waiting for transfers between devices, backward_group(): lax.all_to_all(outgoing, 'expert', split_axis=0, concat_axis=0, tiled=True)  120 us
    ppermute x2, waiting for transfers between devices, passed_along(): lax.ppermute(value, axis, [(source, source + steps) for source in range(f...  63.9 us
    all_to_all x2, waiting for transfers between devices, forward_group(): lax.all_to_all(outgoing, 'expert', split_axis=0, concat_axis=0, tiled=True)  42.6 us
    all_to_all x2, waiting for transfers between devices, backward_group(): lax.all_to_all(partial_value.astype(jnp.bfloat16), 'expert', split_axis=0...  29.8 us
    another operation x4, local copies, waits for them, and re-layouts, backward_group(): pack_slots(joined, target, experts, capacity)  22.1 us
    all_to_all x2, waiting for transfers between devices, forward_group(): lax.all_to_all(partial_value.astype(jnp.bfloat16), 'expert', split_axis=0...  19.2 us
    dot_general x2, matrix products, expert_forward(): jnp.einsum('nch,hd->ncd', hidden, w_down, preferred_element_type=jnp.floa...  17.6 us
    all_to_all x2, starting transfers between devices, forward_group(): lax.all_to_all(outgoing, 'expert', split_axis=0, concat_axis=0, tiled=True)  14.9 us
  transfers between devices with their start and end apart: 12, of which 9 were waited for; matrix products, arithmetic and copies ran while one was open for 23% of the time, Pallas kernels for 0%

commit v1 on v0

v1 whole, which is shorter than its diff:
```python
import functools
from typing import Any, NamedTuple

import jax
import jax.numpy as jnp
from jax import lax
from jax.experimental import pallas as pl
from jax.experimental.pallas import tpu as pltpu
from jax.sharding import PartitionSpec as P

NORM_EPS = 1e-06
ROUTE_SCALE = 2.5
MESH = pl.DeviceIdType.MESH
F32 = jnp.float32
BF16 = jnp.bfloat16
CHUNKS = 7
LINE = 4
AHEAD = 4


def dot(a, b):
    return jnp.dot(a, b, preferred_element_type=F32)


def dot_t(a, b):
    return lax.dot_general(a, b, (((1,), (1,)), ((), ())), preferred_element_type=F32)


def iota(shape, axis):
    return lax.broadcasted_iota(jnp.int32, shape, axis)


def split_dot(weights, values):
    high = weights.astype(BF16)
    low = (weights - high.astype(F32)).astype(BF16)
    return dot(high, values) + dot(low, values)


class Move:
    def __init__(self, src, dst, send, recv, device):
        self.copy = pltpu.make_async_remote_copy(
            src_ref=src, dst_ref=dst, send_sem=send, recv_sem=recv,
            device_id=device, device_id_type=MESH,
        )

    def start(self):
        self.copy.start()

    def recv(self):
        self.copy.wait_recv()

    def sent(self):
        self.copy.wait_send()


class Refs(NamedTuple):
    act: Any
    grad: Any
    feed: Any
    loss: Any
    saved: Any
    fgain: Any
    bgain: Any
    frouter: Any
    brouter: Any
    fgate: Any
    fup: Any
    fdown: Any
    bgate: Any
    bup: Any
    bdown: Any
    ids: Any
    out_f: Any
    out_b: Any
    xf0: Any
    xf1: Any
    xc: Any
    xs: Any
    tf: Any
    tn: Any
    pkf: Any
    pkn: Any
    pkc: Any
    rf: Any
    rn: Any
    rc: Any
    sf: Any
    sg: Any
    pf: Any
    pg: Any
    xif: Any
    xig: Any
    ysf: Any
    ysg: Any
    yrf: Any
    yrg: Any
    owf: Any
    owg: Any
    of: Any
    ob: Any
    wfg: Any
    wfu: Any
    wfd: Any
    wbg: Any
    wbu: Any
    wbd: Any
    ag: Any
    au: Any
    bg: Any
    bu: Any
    bh: Any
    hidden: Any
    gg: Any
    ug: Any
    seall: Any
    sep: Any
    ser: Any
    sex: Any
    sei: Any
    seys: Any
    seyr: Any
    seown: Any
    gaf: Any
    gan: Any
    rsn: Any
    idb: Any
    idall: Any
    idsend: Any
    idtb: Any
    ld_w: Any
    ld_x: Any
    ld_out: Any
    ysem_s: Any
    ysem_r: Any
    xsem_s: Any
    xsem_r: Any
    dsem_s: Any
    dsem_r: Any
    d2_s: Any
    d2_r: Any
    x2_s: Any
    x2_r: Any
    y2_s: Any
    y2_r: Any
    hop_s: Any
    hop_r: Any
    fy_s: Any
    sd_s: Any
    sd_r: Any
    sx_s: Any
    sx_r: Any
    sy_s: Any
    sy_r: Any
    id_s: Any
    id_r: Any


def kernel(dims, *refs):
    rows, width, cap, hid, sections = dims
    nc = CHUNKS
    cw = width // nc
    slots = 2 * cap
    line_rows = LINE * slots
    g = Refs(*refs)

    sec = lax.axis_index("section")
    me = lax.axis_index("expert")
    core = lax.rem(me, 2)
    x = lax.rem(me // 2, LINE)
    y = me // (2 * LINE)
    mate_index = lax.rem(me + 2 * LINE, 4 * LINE)
    sibling = (sec, me + 1 - 2 * core)
    mate = (sec, mate_index)

    def along(step):
        return (sec, (y * LINE + lax.rem(x + step, LINE)) * 2 + core)

    next_sec = lax.rem(sec + 1, sections)
    last_sec = lax.rem(sec + sections - 1, sections)
    first = sec == 0
    inner = sec != 0
    sender = sec != sections - 1
    own_rows = pl.ds(0, rows)
    mate_rows = pl.ds(rows, rows)
    own_part = pl.ds(0, line_rows)
    sibling_part = pl.ds(line_rows, line_rows)

    def cols(ch):
        return pl.ds(pl.multiple_of(ch * cw, cw), cw)

    def chunks(*bodies):
        @pl.loop(0, nc)
        def _(ch):
            for body in bodies:
                body(ch)

    loads = (
        (g.grad, g.xc.at[0, :, own_rows]), (g.saved.at[0], g.xs.at[0]), (g.act, g.xf0),
        (g.saved.at[1], g.xs.at[1]), (g.loss, g.xc.at[1, :, own_rows]), (g.feed, g.xf1.at[:, own_rows]),
    )
    cot_0, saved_0, act_0, saved_1, cot_1, act_1 = range(6)

    def load_start(k):
        src, dst = loads[k]
        chunks(lambda ch: pltpu.make_async_copy(src.at[:, cols(ch)], dst.at[ch], g.ld_x.at[k]).start())

    def load_wait(k):
        dst = loads[k][1]
        pltpu.make_async_copy(dst, dst, g.ld_x.at[k]).wait()

    weights = [
        pltpu.make_async_copy(src, dst, g.ld_w.at[k])
        for k, (src, dst) in enumerate((
            (g.bdown, g.wbd), (g.bgate, g.wbg), (g.bup, g.wbu),
            (g.fgate, g.wfg), (g.fup, g.wfu), (g.fdown, g.wfd),
        ))
    ]
    load_bdown, load_bgate, load_bup, load_fgate, load_fup, load_fdown = weights

    for k in (cot_0, saved_0, act_0, saved_1):
        load_start(k)

    @pl.when(first)
    def _():
        load_start(cot_1)
        load_start(act_1)

    for copy in weights:
        copy.start()

    barrier = pltpu.get_barrier_semaphore()
    partners = [sibling, mate] + [along(d) for d in (1, 2, 3)]
    partners += [(s, e) for s in (next_sec, last_sec) for e in (me, mate_index)]
    for device in partners:
        pl.semaphore_signal(barrier, inc=1, device_id=device, device_id_type=MESH)
    pl.semaphore_wait(barrier, len(partners))

    g.idsend[...] = pltpu.roll(g.ids[...], rows, 1)
    id_move = Move(g.idsend, g.idtb, g.id_s.at[0], g.id_r.at[0], mate)
    id_move.start()

    blocks = (g.tf, g.tn.at[0], g.tn.at[1], g.xc.at[0])
    packs = (g.pkf, g.pkn, g.pkn, g.pkc)
    arrivals = (g.rf, g.rn, g.rn, g.rc)

    shared_sem = (0, 1, 1, 2)
    far = pl.ds(slots, 3 * slots)

    def y_move(p, ch):
        t = blocks[p]
        return Move(t.at[ch, own_rows], t.at[ch, mate_rows], g.ysem_s.at[p], g.ysem_r.at[p, ch], mate)

    def x_move(p, ch, d):
        return Move(
            packs[p].at[ch, pl.ds((d - 1) * slots, slots)], arrivals[p].at[ch, pl.ds(d * slots, slots)],
            g.xsem_s.at[shared_sem[p]], g.xsem_r.at[shared_sem[p], ch], along(d),
        )

    def d_move(p, ch):
        r = arrivals[p]
        k = shared_sem[p]
        return Move(r.at[ch, own_part], r.at[ch, sibling_part], g.dsem_s.at[k], g.dsem_r.at[k, ch], sibling)

    def y_sent(p):
        block = blocks[p].at[:, own_rows]
        Move(block, block, g.ysem_s.at[p], g.ysem_r.at[p, 0], mate).sent()

    def packed_sent(p):
        k = shared_sem[p]
        Move(packs[p], packs[p], g.xsem_s.at[k], g.xsem_r.at[k, 0], mate).sent()

    def shared_sent(p):
        k = shared_sem[p]
        block = arrivals[p].at[:, own_part]
        Move(block, block, g.dsem_s.at[k], g.dsem_r.at[k, 0], sibling).sent()

    def y_recv(p):
        return lambda ch: y_move(p, ch).recv()

    def y_ahead(p, later):
        def body(ch):
            @pl.when(ch < nc - AHEAD)
            def _():
                y_move(p, ch + AHEAD).start()
            if later is not None:
                @pl.when(ch >= nc - AHEAD)
                def _():
                    y_move(later, ch + AHEAD - nc).start()
        return body

    def pack(p, block, placer):
        def body(ch):
            packed = dot(placer, block[ch]).astype(BF16)
            packs[p][ch] = packed[slots:]
            for d in (2, 1, 3):
                x_move(p, ch, d).start()
            arrivals[p][ch, 0:slots] = packed[0:slots]
        return body

    def share(p):
        def body(ch):
            k = shared_sem[p]
            block = arrivals[p].at[ch, far]
            Move(block, block, g.xsem_s.at[k], g.xsem_r.at[k, ch], mate).recv()
            d_move(p, ch).start()
        return body

    def norm_rows(load_chunk, gain, store_chunk):
        wide = [load_chunk(ch).astype(F32) for ch in range(nc)]
        total = sum(jnp.sum(v * v, axis=1, keepdims=True) for v in wide)
        inv_rms = lax.rsqrt(total / width + NORM_EPS)
        for ch, v in enumerate(wide):
            store_chunk(ch, (v * inv_rms * gain[:, ch * cw:(ch + 1) * cw]).astype(BF16))
        return inv_rms

    def packer(column):
        shape = (line_rows, 2 * rows)
        row, token = iota(shape, 0), iota(shape, 1)
        expert = y * LINE + lax.rem(x + row // slots, LINE)
        both = g.idall[...]
        named = (both[column:column + 1] == expert) | (both[column + 1:column + 2] == expert)
        up = (2 * rows, 2 * rows)
        tri = (iota(up, 0) < iota(up, 1)) & (iota(up, 0) // rows == iota(up, 1) // rows)
        place = dot(named.astype(F32).astype(BF16), tri.astype(F32).astype(BF16))
        within = lax.rem(row, slots)
        hit = named & (place == lax.rem(within, cap).astype(F32)) & (within // cap == token // rows)
        return hit.astype(F32).astype(BF16)

    def unpacker(column):
        shape = (2 * rows, line_rows)
        token, col = iota(shape, 0), iota(shape, 1)
        expert = y * LINE + lax.rem(x + col // slots, LINE)
        ids = g.idb[...]
        named0 = ids[:, column:column + 1] == expert
        named1 = ids[:, column + 1:column + 2] == expert
        low = (2 * rows, 2 * rows)
        tri = (iota(low, 1) < iota(low, 0)) & (iota(low, 0) // rows == iota(low, 1) // rows)
        place = dot(tri.astype(F32).astype(BF16), (named0 | named1).astype(F32).astype(BF16))
        within = lax.rem(col, slots)
        fits = (place == lax.rem(within, cap).astype(F32)) & (within // cap == token // rows)
        return (fits & named0).astype(F32), (fits & named1).astype(F32)

    def gating(t, router, column, store):
        logits = sum(dot_t(t[ch], router[:, ch * cw:(ch + 1) * cw]) for ch in range(nc))
        ids = g.idb[...]
        experts = iota(logits.shape, 1)
        aff = []
        for k in range(2):
            picked = jnp.where(ids[:, column + k:column + k + 1] == experts, logits, 0.0)
            aff.append(jax.nn.sigmoid(jnp.sum(picked, axis=1, keepdims=True)))
        total = aff[0] + aff[1]
        lane = iota((2 * rows, 128), 1)
        value = jnp.where(lane == 0, aff[0], jnp.where(lane == 1, aff[1], 0.0))
        value = jnp.where(lane == 2, ROUTE_SCALE * aff[0] / total, value)
        store[...] = jnp.where(lane == 3, ROUTE_SCALE * aff[1] / total, value)

    def gather_up(p, w_gate, w_up, acc_g, acc_u):
        def body(ch):
            d_move(p, ch).recv()
            acc_g[...] += dot(arrivals[p][ch], w_gate[cols(ch)])
            acc_u[...] += dot(arrivals[p][ch], w_up[cols(ch)])
        return body

    def gather_grad(ch):
        d_move(3, ch).recv()
        g.bh[...] += dot_t(g.rc[ch], g.wbd[:, cols(ch)])

    partial = (g.pf, g.pg)
    from_sibling = (g.sf, g.sg)
    returned = (g.xif, g.xig)
    own_sum = (g.owf, g.owg)
    to_mate = (g.ysf, g.ysg)
    from_mate = (g.yrf, g.yrg)
    results = (g.of, g.ob)
    inboxes = (g.xf1, g.xc.at[1])
    outs = (g.out_f, g.out_b)

    def d2_move(q, ch):
        return Move(partial[q].at[ch], from_sibling[q].at[ch], g.d2_s.at[q], g.d2_r.at[q, ch], sibling)

    def x2_move(q, ch, d):
        part = pl.ds(d * slots, slots)
        return Move(
            partial[q].at[ch, part], returned[q].at[ch, part],
            g.x2_s.at[q], g.x2_r.at[q, ch], along(LINE - d),
        )

    def y2_move(q, ch):
        return Move(to_mate[q].at[ch], from_mate[q].at[ch], g.y2_s.at[q], g.y2_r.at[q, ch], mate)

    def product(q, part, ch):
        if q == 0:
            return dot(g.hidden[part], g.wfd[:, cols(ch)])
        return dot_t(g.gg[part], g.wbg[cols(ch)]) + dot_t(g.ug[part], g.wbu[cols(ch)])

    def half_out(q):
        def body(ch):
            partial[q][ch] = product(q, sibling_part, ch).astype(BF16)
            d2_move(q, ch).start()
        return body

    def half_sent(q, payloads):
        Move(partial[q], partial[q], g.d2_s.at[q], g.d2_r.at[q, 0], sibling).sent()
        for p in payloads:
            shared_sent(p)

    def half_own(q):
        def body(ch):
            value = product(q, own_part, ch)
            d2_move(q, ch).recv()
            partial[q][ch] = (value + from_sibling[q][ch].astype(F32)).astype(BF16)
            for d in (2, 1, 3):
                x2_move(q, ch, d).start()
            returned[q][ch, 0:slots] = partial[q][ch, 0:slots]
        return body

    def combine(q, mix):
        def body(ch):
            block = returned[q].at[ch, far]
            Move(block, block, g.x2_s.at[q], g.x2_r.at[q, ch], mate).recv()
            mixed = split_dot(mix, returned[q][ch])
            own_sum[q][ch] = mixed[0:rows]
            to_mate[q][ch] = mixed[rows:].astype(BF16)
            y2_move(q, ch).start()
        return body

    def return_sent(q):
        block = partial[q].at[:, far]
        Move(block, block, g.x2_s.at[q], g.x2_r.at[q, 0], mate).sent()
        Move(to_mate[q], to_mate[q], g.y2_s.at[q], g.y2_r.at[q, 0], mate).sent()

    def hop_move(q, ch, other):
        target = (next_sec, mate_index if other else me)
        part = mate_rows if other else own_rows
        return Move(
            results[q].at[0, ch], inboxes[q].at[ch, part],
            g.hop_s.at[q, other], g.hop_r.at[q, other, ch], target,
        )

    def feed_move(q, ch):
        return Move(
            inboxes[q].at[ch, own_rows], inboxes[q].at[ch, mate_rows],
            g.fy_s.at[q], g.hop_r.at[q, 1, ch], mate,
        )

    def out_copy(q, tick, ch):
        return pltpu.make_async_copy(results[q].at[tick, ch], outs[q].at[tick, :, cols(ch)], g.ld_out.at[q])

    def deliver(q, tick, ch):
        if tick == 0:
            @pl.when(sender)
            def _():
                for other in (0, 1):
                    hop_move(q, ch, other).start()
        out_copy(q, tick, ch).start()

    def arrived(q):
        def body(ch):
            @pl.when(inner)
            def _():
                hop_move(q, ch, 0).recv()
            hop_move(q, ch, 1).recv()
        return body

    def sens_d():
        return Move(g.sep, g.ser, g.sd_s.at[0], g.sd_r.at[0], sibling)

    def sens_x(d):
        part = pl.ds(d * slots, slots)
        return Move(g.sex.at[part], g.sei.at[part], g.sx_s.at[0], g.sx_r.at[0], along(LINE - d))

    def sens_y():
        return Move(g.seys, g.seyr, g.sy_s.at[0], g.sy_r.at[0], mate)

    def mix_of(store, column):
        hit0, hit1 = unpacker(column)
        return hit0 * store[:, 2:3] + hit1 * store[:, 3:4], hit0, hit1

    def activate():
        @pl.loop(0, 2 * LINE)
        def _(n):
            part = pl.ds(pl.multiple_of(n * slots, 16), slots)
            pre = g.ag[part]
            g.hidden[part] = (pre * jax.nn.sigmoid(pre) * g.au[part]).astype(BF16)

    def forward_finish(tick):
        before = g.xf0 if tick == 0 else g.xf1

        def body(ch):
            y2_move(0, ch).recv()
            value = before[ch, 0:rows].astype(F32) + (g.owf[ch] + g.yrf[ch].astype(F32))
            g.of[tick, ch] = value.astype(BF16)
            deliver(0, tick, ch)
        chunks(body)

    def backward_act():
        @pl.loop(0, 2 * LINE)
        def _(n):
            part = pl.ds(pl.multiple_of(n * slots, 16), slots)
            pre, up, hgrad = g.bg[part], g.bu[part], g.bh[part]
            sig = jax.nn.sigmoid(pre)
            silu = pre * sig
            act = (silu * up).astype(BF16).astype(F32)
            sens = jnp.sum(act * hgrad, axis=1, keepdims=True)
            g.gg[part] = (hgrad * up * sig * (1.0 + pre * (1.0 - sig))).astype(BF16)
            g.ug[part] = (hgrad * silu).astype(BF16)
            g.seall[part] = jnp.broadcast_to(sens, (slots, 128))
        g.sep[...] = g.seall[line_rows:]
        sens_d().start()

    def sens_out():
        sens_d().sent()
        sens_d().recv()
        g.sex[...] = g.seall[0:line_rows] + g.ser[...]
        for d in (1, 2, 3):
            sens_x(d).start()
        g.sei[0:slots] = g.sex[0:slots]

    def sens_combine(hits):
        block = g.sei.at[far]
        Move(block, block, g.sx_s.at[0], g.sx_r.at[0], mate).recv()
        found = [
            jnp.dot(hit, g.sei[...], precision=lax.Precision.HIGHEST, preferred_element_type=F32)
            for hit in hits
        ]
        lane = iota((2 * rows, 128), 1)
        both = jnp.where(lane == 0, found[0], jnp.where(lane == 1, found[1], 0.0))
        g.seown[...] = both[0:rows]
        g.seys[...] = both[rows:]
        sens_y().start()

    def sens_sent():
        block = g.sex.at[far]
        Move(block, block, g.sx_s.at[0], g.sx_r.at[0], mate).sent()
        sens_y().sent()

    def backward_finish(tick):
        sens_y().recv()
        sens = g.seown[...] + g.seyr[...]
        store = g.gan.at[tick]
        aff = [store[0:rows, k:k + 1] for k in range(2)]
        total = aff[0] + aff[1]
        weighted = aff[0] * sens[:, 0:1] + aff[1] * sens[:, 1:2]
        column = 4 + 2 * tick
        ids = g.idb[0:rows]
        experts = iota((rows, 8), 1)
        spread = jnp.zeros((rows, 8), F32)
        for k in range(2):
            lgrad = ROUTE_SCALE / total * (sens[:, k:k + 1] - weighted / total) * aff[k] * (1.0 - aff[k])
            spread = spread + jnp.where(ids[:, column + k:column + k + 1] == experts, lgrad, 0.0)
        high = spread.astype(BF16)
        rest = spread - high.astype(F32)
        mid = rest.astype(BF16)
        low = (rest - mid.astype(F32)).astype(BF16)

        def gather(ch, inner_sum):
            router = g.brouter[:, cols(ch)]
            y2_move(1, ch).recv()
            ngrad = g.owg[ch] + g.yrg[ch].astype(F32)
            ngrad = ngrad + (dot(high, router) + dot(mid, router) + dot(low, router))
            scaled = g.bgain[:, cols(ch)] * ngrad
            g.owg[ch] = scaled
            return inner_sum + jnp.sum(g.xs[tick, ch].astype(F32) * scaled, axis=1, keepdims=True)

        inner_sum = lax.fori_loop(0, nc, gather, jnp.zeros((rows, 1), F32))
        inv_rms = g.rsn[tick][:, 0:1]
        factor = inv_rms * inv_rms * inv_rms * (inner_sum / width)

        def body(ch):
            value = g.xc[tick, ch, 0:rows].astype(F32) + inv_rms * g.owg[ch]
            value = value - g.xs[tick, ch].astype(F32) * factor
            g.ob[tick, ch] = value.astype(BF16)
            deliver(1, tick, ch)
        chunks(body)

    def clear(*sums):
        for ref in sums:
            ref[...] = jnp.zeros_like(ref)

    def norm_saved(tick):
        def store(ch, value):
            g.tn[tick, ch, 0:rows] = value
        inv_rms = norm_rows(lambda ch: g.xs[tick, ch], g.bgain, store)
        g.rsn[tick] = jnp.broadcast_to(inv_rms, (rows, 128))

    def norm_forward(block, base):
        def store(ch, value):
            g.tf[ch, base:base + rows] = value
        norm_rows(lambda ch: block[ch, base:base + rows], g.fgain, store)

    load_wait(cot_0)
    for ch in range(AHEAD):
        y_move(3, ch).start()
    id_move.recv()
    g.idall[...] = jnp.maximum(g.ids[...], g.idtb[...])
    g.idb[...] = g.idall[...].T
    placer_b = packer(4)
    load_wait(saved_0)
    norm_saved(0)
    chunks(y_recv(3), y_ahead(3, 1), pack(3, g.xc.at[0], placer_b))
    load_wait(act_0)
    norm_forward(g.xf0, 0)
    clear(g.bh, g.bg, g.bu, g.ag, g.au)
    chunks(y_recv(1), y_ahead(1, 0), pack(1, g.tn.at[0], placer_b), share(3))
    load_wait(saved_1)
    norm_saved(1)
    placer_f = packer(0)
    load_bdown.wait()
    chunks(y_recv(0), y_ahead(0, 2), share(1), pack(0, g.tf, placer_f), gather_grad)
    gating(g.tn.at[0], g.brouter, 4, g.gan.at[0])
    for ch in range(AHEAD, nc):
        y_move(2, ch).start()

    @pl.when(first)
    def _():
        for q, k in ((1, cot_1), (0, act_1)):
            load_wait(k)
            chunks(lambda ch, q=q: feed_move(q, ch).start())

    for tick in range(2):
        if tick == 0:
            load_bgate.wait()
            load_bup.wait()
            chunks(gather_up(1, g.wbg, g.wbu, g.bg, g.bu))
        backward_act()
        chunks(half_out(1))
        sens_out()
        half_sent(1, (1 + tick, 3))
        chunks(half_own(1), share(0))
        if tick == 0:
            gating(g.tf, g.frouter, 0, g.gaf)
            load_fgate.wait()
            load_fup.wait()
        chunks(gather_up(0, g.wfg, g.wfu, g.ag, g.au))
        activate()
        if tick == 0:
            load_fdown.wait()
        chunks(half_out(0))
        mix, hit0, hit1 = mix_of(g.gan.at[tick], 4 + 2 * tick)
        sens_combine((hit0, hit1))
        half_sent(0, (0,))
        chunks(combine(1, mix), half_own(0))
        backward_finish(tick)
        mix, _, _ = mix_of(g.gaf, 2 * tick)
        if tick == 1:
            chunks(combine(0, mix))
            forward_finish(1)
            break
        placer_b = packer(6)
        packed_sent(1)
        clear(g.bh, g.bg, g.bu, g.ag, g.au)
        chunks(combine(0, mix), y_recv(2), pack(2, g.tn.at[1], placer_b))
        forward_finish(0)
        packed_sent(3)
        packed_sent(0)
        return_sent(0)
        return_sent(1)
        y_sent(0)
        sens_sent()
        chunks(arrived(1), pack(3, g.xc.at[1], placer_b), share(2))
        gating(g.tn.at[1], g.brouter, 6, g.gan.at[1])
        chunks(gather_up(2, g.wbg, g.wbu, g.bg, g.bu))
        chunks(arrived(0))
        norm_forward(g.xf1, 0)
        norm_forward(g.xf1, rows)
        placer_f = packer(2)
        chunks(pack(0, g.tf, placer_f), share(3))
        gating(g.tf, g.frouter, 2, g.gaf)
        chunks(gather_grad)

    for p in (0, 2, 3):
        packed_sent(p)
    for p in (1, 2, 3):
        y_sent(p)
    return_sent(0)
    return_sent(1)
    sens_sent()
    id_move.sent()

    @pl.when(sender)
    def _():
        for q in range(2):
            for other in range(2):
                block = results[q].at[0]
                Move(block, block, g.hop_s.at[q, other], g.hop_r.at[q, other, 0], mate).sent()

    @pl.when(first)
    def _():
        for q in range(2):
            block = inboxes[q].at[:, own_rows]
            Move(block, block, g.fy_s.at[q], g.hop_r.at[q, 1, 0], mate).sent()

    for q in range(2):
        pltpu.make_async_copy(results[q], results[q], g.ld_out.at[q]).wait()


def copy_kernel(a, b, out_a, out_b, held, sems):
    moves = [
        (src.at[tick], held.at[2 * k + tick], dst.at[tick], 2 * k + tick)
        for k, (src, dst) in enumerate(((a, out_a), (b, out_b))) for tick in range(2)
    ]
    into = [pltpu.make_async_copy(src, slot, sems.at[0, n]) for src, slot, dst, n in moves]
    back = [pltpu.make_async_copy(slot, dst, sems.at[1, n]) for src, slot, dst, n in moves]
    for copy in into:
        copy.start()
    for first_leg, second_leg in zip(into, back):
        first_leg.wait()
        second_leg.start()
    for copy in back:
        copy.wait()


def per_device(
    act_in, grad_in, feed, loss_grad, saved,
    fwd_gain, fwd_router, fwd_gate, fwd_up, fwd_down,
    bwd_gain, bwd_router, bwd_gate, bwd_up, bwd_down,
    fwd_routes, bwd_routes,
):
    rows, width = act_in.shape[1:]
    hid = fwd_gate.shape[2]
    experts = fwd_router.shape[2]
    cap = rows * fwd_routes.shape[3] // experts + rows // 8
    sections = lax.axis_size("section")
    nc = CHUNKS
    cw = width // nc
    slots = 2 * cap
    line = LINE * slots

    ids = jnp.concatenate([fwd_routes[0], bwd_routes[0]]).transpose(0, 2, 1).reshape(8, rows)
    ids = jnp.pad(ids, ((0, 0), (0, rows)), constant_values=-1)

    any_spec = pl.BlockSpec(memory_space=pl.ANY)
    vmem_spec = pl.BlockSpec(memory_space=pltpu.VMEM)

    def b(*shape):
        return pltpu.VMEM(shape, BF16)

    def f(*shape):
        return pltpu.VMEM(shape, F32)

    def i(*shape):
        return pltpu.VMEM(shape, jnp.int32)

    def dma(*shape):
        return pltpu.SemaphoreType.DMA(shape)

    scratch = [
        b(nc, rows, cw), b(nc, 2 * rows, cw), b(2, nc, 2 * rows, cw), b(2, nc, rows, cw),
        b(nc, 2 * rows, cw), b(2, nc, 2 * rows, cw),
        b(nc, 3 * slots, cw), b(nc, 3 * slots, cw), b(nc, 3 * slots, cw),
        b(nc, 2 * line, cw), b(nc, 2 * line, cw), b(nc, 2 * line, cw),
        b(nc, line, cw), b(nc, line, cw), b(nc, line, cw), b(nc, line, cw),
        b(nc, line, cw), b(nc, line, cw),
        b(nc, rows, cw), b(nc, rows, cw), b(nc, rows, cw), b(nc, rows, cw),
        f(nc, rows, cw), f(nc, rows, cw),
        b(2, nc, rows, cw), b(2, nc, rows, cw),
        b(width, hid), b(width, hid), b(hid, width),
        b(width, hid), b(width, hid), b(hid, width),
        f(2 * line, hid), f(2 * line, hid), f(2 * line, hid), f(2 * line, hid), f(2 * line, hid),
        b(2 * line, hid), b(2 * line, hid), b(2 * line, hid),
        f(2 * line, 128),
        f(line, 128), f(line, 128), f(line, 128), f(line, 128),
        f(rows, 128), f(rows, 128), f(rows, 128),
        f(2 * rows, 128), f(2, 2 * rows, 128), f(2, rows, 128),
        i(2 * rows, 8), i(8, 2 * rows), i(8, 2 * rows), i(8, 2 * rows),
        dma(6), dma(6), dma(2),
        dma(4), dma(4, nc), dma(3), dma(3, nc), dma(3), dma(3, nc),
        dma(2), dma(2, nc), dma(2), dma(2, nc), dma(2), dma(2, nc),
        dma(2, 2), dma(2, 2, nc), dma(2),
        dma(1), dma(1), dma(1), dma(1), dma(1), dma(1), dma(1), dma(1),
    ]
    out_shape = jax.ShapeDtypeStruct((2, rows, width), BF16)
    call = pl.pallas_call(
        functools.partial(kernel, (rows, width, cap, hid, sections)),
        out_shape=(out_shape, out_shape),
        in_specs=[any_spec] * 5 + [vmem_spec] * 4 + [any_spec] * 6 + [vmem_spec],
        out_specs=(any_spec, any_spec),
        scratch_shapes=scratch,
        compiler_params=pltpu.CompilerParams(
            collective_id=0, has_side_effects=True, vmem_limit_bytes=63 * 2**20
        ),
    )
    out_f, out_b = call(
        act_in[0], grad_in[0], feed[0], loss_grad[0], saved[0],
        fwd_gain, bwd_gain, fwd_router[0].T, bwd_router[0].T,
        fwd_gate[0], fwd_up[0], fwd_down[0], bwd_gate[0], bwd_up[0], bwd_down[0],
        ids,
    )
    out_f, out_b = pl.pallas_call(
        copy_kernel,
        out_shape=(out_shape, out_shape),
        in_specs=[any_spec] * 2,
        out_specs=(any_spec, any_spec),
        scratch_shapes=[b(4, rows, width), dma(2, 4)],
    )(out_f, out_b)
    return out_f[None], out_b[None]


def solution(mesh):
    in_specs = (
        P("section", "expert", None),
        P("section", "expert", None),
        P(None, "expert", None),
        P(None, "expert", None),
        P("section", None, "expert", None),
        P("section", None),
        P("section", None, None),
        P("section", None, "expert"),
        P("section", None, "expert"),
        P("section", "expert", None),
        P("section", None),
        P("section", None, None),
        P("section", None, "expert"),
        P("section", None, "expert"),
        P("section", "expert", None),
        P("section", None, "expert", None),
        P("section", None, "expert", None),
    )
    out_specs = (P("section", None, "expert", None), P("section", None, "expert", None))
    return jax.shard_map(
        per_device, mesh=mesh, in_specs=in_specs, out_specs=out_specs, check_vma=False
    )
```

time: 549 us -> 178 us (0.32); the launches traced: 538 us -> 175 us
  waiting for transfers between devices: 280 us -> 0 us
  Pallas kernels: 0 us -> 173 us
  matrix products: 74 us -> 0 us
  starting transfers between devices: 70.8 us -> 0 us
  local copies, waits for them, and re-layouts: 68.4 us -> 0.6 us
  other arithmetic: 43.2 us -> 0.7 us
    all_to_all x10 -> x0, waiting for transfers between devices: 216 us -> none  [the longest x2 120 us: backward_group(): lax.all_to_all(outgoing, 'expert', split_axis=0, concat_axis=0, tiled=True)]
    pallas_call x0 -> x2, Pallas kernels: none -> 173 us  [the longest x1 171 us: per_device(): call(act_in[0], grad_in[0], feed[0], loss_grad[0], saved[0], fwd_gain, bw...]
    dot_general x24 -> x0, matrix products: 74 us -> none  [the longest x2 17.6 us: expert_forward(): jnp.einsum('nch,hd->ncd', hidden, w_down, preferred_element_type=jnp.floa...]
    all_to_all x10 -> x0, starting transfers between devices: 65.4 us -> none  [the longest x2 14.9 us: forward_group(): lax.all_to_all(outgoing, 'expert', split_axis=0, concat_axis=0, tiled=True)]
    ppermute x2 -> x0, waiting for transfers between devices: 63.9 us -> none  [passed_along(): lax.ppermute(value, axis, [(source, source + steps) for source in range(f...]
    reduce_sum x22 -> x0, other arithmetic: 29 us -> none  [the longest x2 8.18 us: backward_group(): normed_grad = jnp.sum(gates[:, :, None] * part_slots, axis=1)]
    another operation x4 -> x0, local copies, waits for them, and re-layouts: 22.1 us -> none  [backward_group(): pack_slots(joined, target, experts, capacity)]
    gather x26 -> x0, local copies, waits for them, and re-layouts: 13.7 us -> none  [the longest x20 5.81 us: gating(): affinity = jax.nn.sigmoid(jnp.take_along_axis(logits, route_ids, axis=1))]
  transfers between devices with their start and end apart: 12 -> 0, of which waited for: 9 -> 0; matrix products, arithmetic and copies ran while one was open for 23% -> 0% of each run, Pallas kernels for 0% -> 0%
where the time goes in v1:
time: 178 us; the launch traced here: 175 us
  Pallas kernels  173 us (97%)
    pallas_call x1, Pallas kernels, per_device(): call(act_in[0], grad_in[0], feed[0], loss_grad[0], saved[0], fwd_gain, bw...  171 us

profile of v1, /device:TPU:96, one launch (start us, length us, event | category | flops | bytes accessed | tf_op | source)
XLA Modules:
  0.0 174.9 jit_solution(7167135348618007401)
XLA Ops:
  0.6 0.7 pad_add_fusion
  1.3 0.6 pad.4.refs_15_
  1.9 170.6 %shard_map.176 = (bf16[2,64,3584]{2,1,0:T(8,128)(2,1)}, bf16[2,64,3584]{2,1,0:T(8,128)(2,1)}) custom-call(bf16[64,3584]{1,0:T(8,128)(2,1)} %bitcast.31, bf16[64,3584]{1,0:T(8,128)(2,1)} %bitcast.32, bf16[64,3584]{1,0:T(8,128)(2,1)} %bitcast.33, bf16[64,3584]{1,0:T(8,128)(2,1)} %bitcast.34, bf16[2,64,3584]{2,1,0:T(8,128)(2,1)} %bitcast.30, ...), custom_call_target="tpu_custom_call" | custom-call | tf_op jit(solution)/shard_map/pallas_call | solution.py:783
  172.6 2.3 %shard_map.177 = (bf16[2,64,3584]{2,1,0:T(8,128)(2,1)}, bf16[2,64,3584]{2,1,0:T(8,128)(2,1)}) custom-call(bf16[2,64,3584]{2,1,0:T(8,128)(2,1)} %get-tuple-element.6.a, bf16[2,64,3584]{2,1,0:T(8,128)(2,1)} %get-tuple-element.7.b), custom_call_target="tpu_custom_call" | custom-call | tf_op jit(solution)/shard_map/pallas_call | solution.py:789

commit v2 on v1

--- a/solution.py
+++ b/solution.py
@@ -15,7 +15,8 @@
 BF16 = jnp.bfloat16
 CHUNKS = 7
 LINE = 4
-AHEAD = 4
+AHEAD = 5
+HEAD = CHUNKS - AHEAD
 
 
 def dot(a, b):
@@ -123,6 +124,8 @@
     gaf: Any
     gan: Any
     rsn: Any
+    zs: Any
+    zr: Any
     idb: Any
     idall: Any
     idsend: Any
@@ -153,6 +156,10 @@
     sy_r: Any
     id_s: Any
     id_r: Any
+    ga_s: Any
+    ga_r: Any
+    zsem_s: Any
+    zsem_r: Any
 
 
 def kernel(dims, *refs):
@@ -179,6 +186,8 @@
     last_sec = lax.rem(sec + sections - 1, sections)
     first = sec == 0
     inner = sec != 0
+    even = lax.rem(sec, 2) == 0
+    odd = jnp.logical_not(even)
     sender = sec != sections - 1
     own_rows = pl.ds(0, rows)
     mate_rows = pl.ds(rows, rows)
@@ -188,8 +197,8 @@
     def cols(ch):
         return pl.ds(pl.multiple_of(ch * cw, cw), cw)
 
-    def chunks(*bodies):
-        @pl.loop(0, nc)
+    def chunks(*bodies, start=0, stop=nc):
+        @pl.loop(start, stop)
         def _(ch):
             for body in bodies:
                 body(ch)
@@ -211,33 +220,28 @@
     weights = [
         pltpu.make_async_copy(src, dst, g.ld_w.at[k])
         for k, (src, dst) in enumerate((
-            (g.bdown, g.wbd), (g.bgate, g.wbg), (g.bup, g.wbu),
+            (g.bgate, g.wbg), (g.bup, g.wbu), (g.bdown, g.wbd),
             (g.fgate, g.wfg), (g.fup, g.wfu), (g.fdown, g.wfd),
         ))
     ]
-    load_bdown, load_bgate, load_bup, load_fgate, load_fup, load_fdown = weights
-
-    for k in (cot_0, saved_0, act_0, saved_1):
+    load_bgate, load_bup, load_bdown, load_fgate, load_fup, load_fdown = weights
+
+    for k in (saved_0, cot_0, act_0, saved_1):
         load_start(k)
 
     @pl.when(first)
     def _():
         load_start(cot_1)
         load_start(act_1)
-
-    for copy in weights:
-        copy.start()
 
     barrier = pltpu.get_barrier_semaphore()
     partners = [sibling, mate] + [along(d) for d in (1, 2, 3)]
     partners += [(s, e) for s in (next_sec, last_sec) for e in (me, mate_index)]
     for device in partners:
         pl.semaphore_signal(barrier, inc=1, device_id=device, device_id_type=MESH)
-    pl.semaphore_wait(barrier, len(partners))
 
     g.idsend[...] = pltpu.roll(g.ids[...], rows, 1)
     id_move = Move(g.idsend, g.idtb, g.id_s.at[0], g.id_r.at[0], mate)
-    id_move.start()
 
     blocks = (g.tf, g.tn.at[0], g.tn.at[1], g.xc.at[0])
     packs = (g.pkf, g.pkn, g.pkn, g.pkc)
@@ -249,6 +253,9 @@
     def y_move(p, ch):
         t = blocks[p]
         return Move(t.at[ch, own_rows], t.at[ch, mate_rows], g.ysem_s.at[p], g.ysem_r.at[p, ch], mate)
+
+    def z_move(ch):
+        return Move(g.zs.at[ch], g.zr.at[ch], g.zsem_s.at[0], g.zsem_r.at[ch], mate)
 
     def x_move(p, ch, d):
         return Move(
@@ -262,8 +269,11 @@
         return Move(r.at[ch, own_part], r.at[ch, sibling_part], g.dsem_s.at[k], g.dsem_r.at[k, ch], sibling)
 
     def y_sent(p):
-        block = blocks[p].at[:, own_rows]
+        block = blocks[p].at[pl.ds(HEAD, nc - HEAD) if p == 1 else pl.ds(0, nc), own_rows]
         Move(block, block, g.ysem_s.at[p], g.ysem_r.at[p, 0], mate).sent()
+
+    def z_sent():
+        Move(g.zs, g.zs, g.zsem_s.at[0], g.zsem_r.at[0], mate).sent()
 
     def packed_sent(p):
         k = shared_sem[p]
@@ -297,11 +307,37 @@
             arrivals[p][ch, 0:slots] = packed[0:slots]
         return body
 
+    def x_recv(p, ch):
+        block = arrivals[p].at[ch, far]
+        Move(block, block, g.xsem_s.at[shared_sem[p]], g.xsem_r.at[shared_sem[p], ch], mate).recv()
+
     def share(p):
         def body(ch):
-            k = shared_sem[p]
-            block = arrivals[p].at[ch, far]
-            Move(block, block, g.xsem_s.at[k], g.xsem_r.at[k, ch], mate).recv()
+            x_recv(p, ch)
+            d_move(p, ch).start()
+        return body
+
+    def swap_out(p):
+        shape = (line_rows // 2, line_rows)
+        row, col = iota(shape, 0), iota(shape, 1)
+        other = (col == row // cap * slots + cap + lax.rem(row, cap)).astype(F32).astype(BF16)
+
+        def body(ch):
+            x_recv(p, ch)
+            g.zs[ch] = dot(other, g.rn[ch, 0:line_rows]).astype(BF16)
+            z_move(ch).start()
+        return body
+
+    def swap_in(p):
+        shape = (line_rows, line_rows // 2)
+        row, col = iota(shape, 0), iota(shape, 1)
+        place = (row == col // cap * slots + cap + lax.rem(col, cap)).astype(F32).astype(BF16)
+
+        def body(ch):
+            z_move(ch).recv()
+            swapped = dot(place, g.zr[ch])
+            mine = lax.rem(iota(swapped.shape, 0), slots) < cap
+            g.rn[ch, 0:line_rows] = jnp.where(mine, g.rn[ch, 0:line_rows].astype(F32), swapped).astype(BF16)
             d_move(p, ch).start()
         return body
 
@@ -325,6 +361,19 @@
         within = lax.rem(row, slots)
         hit = named & (place == lax.rem(within, cap).astype(F32)) & (within // cap == token // rows)
         return hit.astype(F32).astype(BF16)
+
+    def own_packer(column):
+        shape = (line_rows, 2 * rows)
+        row, token = iota(shape, 0), iota(shape, 1)
+        within = lax.rem(row, slots)
+        expert = lax.rem(y + within // cap, 2) * LINE + lax.rem(x + row // slots, LINE)
+        ids = g.ids[...]
+        named = (ids[column:column + 1] == expert) | (ids[column + 1:column + 2] == expert)
+        up = (2 * rows, 2 * rows)
+        tri = iota(up, 0) < iota(up, 1)
+        place = dot(named.astype(F32).astype(BF16), tri.astype(F32).astype(BF16))
+        hit = named & (place == lax.rem(within, cap).astype(F32))
+        return hit.astype(F32).astype(BF16)[:, 0:rows]
 
     def unpacker(column):
         shape = (2 * rows, line_rows)
@@ -342,14 +391,15 @@
 
     def gating(t, router, column, store):
         logits = sum(dot_t(t[ch], router[:, ch * cw:(ch + 1) * cw]) for ch in range(nc))
-        ids = g.idb[...]
+        count = logits.shape[0]
+        ids = g.idb[0:count]
         experts = iota(logits.shape, 1)
         aff = []
         for k in range(2):
             picked = jnp.where(ids[:, column + k:column + k + 1] == experts, logits, 0.0)
             aff.append(jax.nn.sigmoid(jnp.sum(picked, axis=1, keepdims=True)))
         total = aff[0] + aff[1]
-        lane = iota((2 * rows, 128), 1)
+        lane = iota((count, 128), 1)
         value = jnp.where(lane == 0, aff[0], jnp.where(lane == 1, aff[1], 0.0))
         value = jnp.where(lane == 2, ROUTE_SCALE * aff[0] / total, value)
         store[...] = jnp.where(lane == 3, ROUTE_SCALE * aff[1] / total, value)
@@ -450,8 +500,11 @@
         if tick == 0:
             @pl.when(sender)
             def _():
-                for other in (0, 1):
-                    hop_move(q, ch, other).start()
+                hop_move(q, ch, 0).start()
+
+            @pl.when(sender & even if q == 0 else sender)
+            def _():
+                hop_move(q, ch, 1).start()
         out_copy(q, tick, ch).start()
 
     def arrived(q):
@@ -459,7 +512,10 @@
             @pl.when(inner)
             def _():
                 hop_move(q, ch, 0).recv()
-            hop_move(q, ch, 1).recv()
+            if q == 1:
+                hop_move(q, ch, 1).recv()
+            else:
+                pl.when(odd)(hop_move(q, ch, 1).recv)
         return body
 
     def sens_d():
@@ -588,46 +644,66 @@
             g.tf[ch, base:base + rows] = value
         norm_rows(lambda ch: block[ch, base:base + rows], g.fgain, store)
 
+    def gate_move(tick):
+        store = g.gan.at[tick]
+        return Move(store.at[own_rows], store.at[mate_rows], g.ga_s.at[tick], g.ga_r.at[tick], mate)
+
+    def gate_saved(tick):
+        gating(g.tn.at[tick, :, own_rows], g.brouter, 4 + 2 * tick, g.gan.at[tick, own_rows])
+        gate_move(tick).start()
+
+    load_wait(saved_0)
+    norm_saved(0)
+    placer_n = own_packer(4)
     load_wait(cot_0)
-    for ch in range(AHEAD):
-        y_move(3, ch).start()
+    pl.semaphore_wait(barrier, len(partners))
+    id_move.start()
+    chunks(lambda ch: y_move(1, ch).start(), start=HEAD)
+    chunks(pack(1, g.tn.at[0, :, own_rows], placer_n), stop=HEAD)
+    for copy in weights:
+        copy.start()
     id_move.recv()
     g.idall[...] = jnp.maximum(g.ids[...], g.idtb[...])
     g.idb[...] = g.idall[...].T
     placer_b = packer(4)
-    load_wait(saved_0)
-    norm_saved(0)
-    chunks(y_recv(3), y_ahead(3, 1), pack(3, g.xc.at[0], placer_b))
+    chunks(
+        y_recv(1), lambda ch: y_move(3, ch - HEAD).start(), pack(1, g.tn.at[0], placer_b), start=HEAD,
+    )
     load_wait(act_0)
     norm_forward(g.xf0, 0)
+    chunks(y_recv(3), y_ahead(3, 0), pack(3, g.xc.at[0], placer_b), swap_out(1), stop=HEAD)
+    chunks(y_recv(3), y_ahead(3, 0), pack(3, g.xc.at[0], placer_b), share(1), start=HEAD)
     clear(g.bh, g.bg, g.bu, g.ag, g.au)
-    chunks(y_recv(1), y_ahead(1, 0), pack(1, g.tn.at[0], placer_b), share(3))
+    placer_f = packer(0)
     load_wait(saved_1)
     norm_saved(1)
-    placer_f = packer(0)
-    load_bdown.wait()
-    chunks(y_recv(0), y_ahead(0, 2), share(1), pack(0, g.tf, placer_f), gather_grad)
-    gating(g.tn.at[0], g.brouter, 4, g.gan.at[0])
+    chunks(swap_in(1), stop=HEAD)
+    load_bgate.wait()
+    load_bup.wait()
+    chunks(
+        y_recv(0), y_ahead(0, 2), share(3), pack(0, g.tf, placer_f),
+        gather_up(1, g.wbg, g.wbu, g.bg, g.bu),
+    )
     for ch in range(AHEAD, nc):
         y_move(2, ch).start()
+    load_bdown.wait()
+    chunks(gather_grad)
 
     @pl.when(first)
     def _():
-        for q, k in ((1, cot_1), (0, act_1)):
-            load_wait(k)
-            chunks(lambda ch, q=q: feed_move(q, ch).start())
+        load_wait(act_1)
+        load_wait(cot_1)
+        chunks(lambda ch: feed_move(1, ch).start())
 
     for tick in range(2):
-        if tick == 0:
-            load_bgate.wait()
-            load_bup.wait()
-            chunks(gather_up(1, g.wbg, g.wbu, g.bg, g.bu))
         backward_act()
         chunks(half_out(1))
         sens_out()
         half_sent(1, (1 + tick, 3))
         chunks(half_own(1), share(0))
         if tick == 0:
+            gate_saved(0)
+            gate_saved(1)
             gating(g.tf, g.frouter, 0, g.gaf)
             load_fgate.wait()
             load_fup.wait()
@@ -636,6 +712,7 @@
         if tick == 0:
             load_fdown.wait()
         chunks(half_out(0))
+        gate_move(tick).recv()
         mix, hit0, hit1 = mix_of(g.gan.at[tick], 4 + 2 * tick)
         sens_combine((hit0, hit1))
         half_sent(0, (0,))
@@ -658,13 +735,19 @@
         y_sent(0)
         sens_sent()
         chunks(arrived(1), pack(3, g.xc.at[1], placer_b), share(2))
-        gating(g.tn.at[1], g.brouter, 6, g.gan.at[1])
-        chunks(gather_up(2, g.wbg, g.wbu, g.bg, g.bu))
         chunks(arrived(0))
         norm_forward(g.xf1, 0)
-        norm_forward(g.xf1, rows)
+
+        @pl.when(even)
+        def _():
+            chunks(lambda ch: y_move(0, ch).start())
+
+        @pl.when(odd)
+        def _():
+            norm_forward(g.xf1, rows)
+
         placer_f = packer(2)
-        chunks(pack(0, g.tf, placer_f), share(3))
+        chunks(lambda ch: pl.when(even)(y_move(0, ch).recv), pack(0, g.tf, placer_f), share(3), gather_up(2, g.wbg, g.wbu, g.bg, g.bu))
         gating(g.tf, g.frouter, 2, g.gaf)
         chunks(gather_grad)
 
@@ -672,23 +755,36 @@
         packed_sent(p)
     for p in (1, 2, 3):
         y_sent(p)
+    z_sent()
+    for tick in range(2):
+        gate_move(tick).sent()
     return_sent(0)
     return_sent(1)
     sens_sent()
     id_move.sent()
 
+    def hop_sent(q, other):
+        block = results[q].at[0]
+        Move(block, block, g.hop_s.at[q, other], g.hop_r.at[q, other, 0], mate).sent()
+
     @pl.when(sender)
     def _():
-        for q in range(2):
-            for other in range(2):
-                block = results[q].at[0]
-                Move(block, block, g.hop_s.at[q, other], g.hop_r.at[q, other, 0], mate).sent()
+        hop_sent(0, 0)
+        hop_sent(1, 0)
+        hop_sent(1, 1)
+
+    @pl.when(sender & even)
+    def _():
+        hop_sent(0, 1)
+
+    @pl.when(even)
+    def _():
+        y_sent(0)
 
     @pl.when(first)
     def _():
-        for q in range(2):
-            block = inboxes[q].at[:, own_rows]
-            Move(block, block, g.fy_s.at[q], g.hop_r.at[q, 1, 0], mate).sent()
+        block = inboxes[1].at[:, own_rows]
+        Move(block, block, g.fy_s.at[1], g.hop_r.at[1, 1, 0], mate).sent()
 
     for q in range(2):
         pltpu.make_async_copy(results[q], results[q], g.ld_out.at[q]).wait()
@@ -762,12 +858,13 @@
         f(line, 128), f(line, 128), f(line, 128), f(line, 128),
         f(rows, 128), f(rows, 128), f(rows, 128),
         f(2 * rows, 128), f(2, 2 * rows, 128), f(2, rows, 128),
+        b(HEAD, line // 2, cw), b(HEAD, line // 2, cw),
         i(2 * rows, 8), i(8, 2 * rows), i(8, 2 * rows), i(8, 2 * rows),
         dma(6), dma(6), dma(2),
         dma(4), dma(4, nc), dma(3), dma(3, nc), dma(3), dma(3, nc),
         dma(2), dma(2, nc), dma(2), dma(2, nc), dma(2), dma(2, nc),
         dma(2, 2), dma(2, 2, nc), dma(2),
-        dma(1), dma(1), dma(1), dma(1), dma(1), dma(1), dma(1), dma(1),
+        dma(1), dma(1), dma(1), dma(1), dma(1), dma(1), dma(1), dma(1), dma(2), dma(2), dma(1), dma(HEAD),
     ]
     out_shape = jax.ShapeDtypeStruct((2, rows, width), BF16)
     call = pl.pallas_call(

time: 178 us -> 174 us (0.978); the launches traced: 175 us -> 174 us
  no operation moved by 1% of the time
where the time goes in v2:
time: 174 us
  Pallas kernels  172 us (99%)
    pallas_call x1, Pallas kernels, per_device(): call(act_in[0], grad_in[0], feed[0], loss_grad[0], saved[0], fwd_gain, bw...  170 us

profile of v2, /device:TPU:96, one launch (start us, length us, event | category | flops | bytes accessed | tf_op | source)
XLA Modules:
  0.0 173.8 jit_solution(14339323004494067901)
XLA Ops:
  0.6 0.7 pad_add_fusion
  1.3 0.6 pad.4.refs_15_
  1.9 169.5 %shard_map.176 = (bf16[2,64,3584]{2,1,0:T(8,128)(2,1)}, bf16[2,64,3584]{2,1,0:T(8,128)(2,1)}) custom-call(bf16[64,3584]{1,0:T(8,128)(2,1)} %bitcast.31, bf16[64,3584]{1,0:T(8,128)(2,1)} %bitcast.32, bf16[64,3584]{1,0:T(8,128)(2,1)} %bitcast.33, bf16[64,3584]{1,0:T(8,128)(2,1)} %bitcast.34, bf16[2,64,3584]{2,1,0:T(8,128)(2,1)} %bitcast.30, ...), custom_call_target="tpu_custom_call" | custom-call | tf_op jit(solution)/shard_map/pallas_call | solution.py:880
  171.5 2.3 %shard_map.177 = (bf16[2,64,3584]{2,1,0:T(8,128)(2,1)}, bf16[2,64,3584]{2,1,0:T(8,128)(2,1)}) custom-call(bf16[2,64,3584]{2,1,0:T(8,128)(2,1)} %get-tuple-element.6.a, bf16[2,64,3584]{2,1,0:T(8,128)(2,1)} %get-tuple-element.7.b), custom_call_target="tpu_custom_call" | custom-call | tf_op jit(solution)/shard_map/pallas_call | solution.py:886

commit v3 on v2

--- a/solution.py
+++ b/solution.py
@@ -60,17 +60,17 @@
     feed: Any
     loss: Any
     saved: Any
-    fgain: Any
-    bgain: Any
-    frouter: Any
-    brouter: Any
+    fgain_in: Any
+    bgain_in: Any
+    frouter_in: Any
+    brouter_in: Any
     fgate: Any
     fup: Any
     fdown: Any
     bgate: Any
     bup: Any
     bdown: Any
-    ids: Any
+    ids_in: Any
     out_f: Any
     out_b: Any
     xf0: Any
@@ -124,6 +124,11 @@
     gaf: Any
     gan: Any
     rsn: Any
+    fgain: Any
+    bgain: Any
+    frouter: Any
+    brouter: Any
+    ids: Any
     zs: Any
     zr: Any
     idb: Any
@@ -160,6 +165,7 @@
     ga_r: Any
     zsem_s: Any
     zsem_r: Any
+    ld_s: Any
 
 
 def kernel(dims, *refs):
@@ -226,8 +232,19 @@
     ]
     load_bgate, load_bup, load_bdown, load_fgate, load_fup, load_fdown = weights
 
+    small = [
+        pltpu.make_async_copy(src, dst, g.ld_s.at[k])
+        for k, (src, dst) in enumerate((
+            (g.ids_in, g.ids), (g.bgain_in, g.bgain), (g.fgain_in, g.fgain),
+            (g.brouter_in, g.brouter), (g.frouter_in, g.frouter),
+        ))
+    ]
+    for copy in small[:2]:
+        copy.start()
     for k in (saved_0, cot_0, act_0, saved_1):
         load_start(k)
+    for copy in small[2:]:
+        copy.start()
 
     @pl.when(first)
     def _():
@@ -240,6 +257,8 @@
     for device in partners:
         pl.semaphore_signal(barrier, inc=1, device_id=device, device_id_type=MESH)
 
+    for copy in small[:2]:
+        copy.wait()
     g.idsend[...] = pltpu.roll(g.ids[...], rows, 1)
     id_move = Move(g.idsend, g.idtb, g.id_s.at[0], g.id_r.at[0], mate)
 
@@ -662,6 +681,8 @@
     chunks(pack(1, g.tn.at[0, :, own_rows], placer_n), stop=HEAD)
     for copy in weights:
         copy.start()
+    for copy in small[2:]:
+        copy.wait()
     id_move.recv()
     g.idall[...] = jnp.maximum(g.ids[...], g.idtb[...])
     g.idb[...] = g.idall[...].T
@@ -735,6 +756,7 @@
         y_sent(0)
         sens_sent()
         chunks(arrived(1), pack(3, g.xc.at[1], placer_b), share(2))
+        chunks(gather_up(2, g.wbg, g.wbu, g.bg, g.bu))
         chunks(arrived(0))
         norm_forward(g.xf1, 0)
 
@@ -747,7 +769,7 @@
             norm_forward(g.xf1, rows)
 
         placer_f = packer(2)
-        chunks(lambda ch: pl.when(even)(y_move(0, ch).recv), pack(0, g.tf, placer_f), share(3), gather_up(2, g.wbg, g.wbu, g.bg, g.bu))
+        chunks(lambda ch: pl.when(even)(y_move(0, ch).recv), pack(0, g.tf, placer_f), share(3))
         gating(g.tf, g.frouter, 2, g.gaf)
         chunks(gather_grad)
 
@@ -791,9 +813,11 @@
 
 
 def copy_kernel(a, b, out_a, out_b, held, sems):
+    half = a.shape[1] // 2
     moves = [
-        (src.at[tick], held.at[2 * k + tick], dst.at[tick], 2 * k + tick)
-        for k, (src, dst) in enumerate(((a, out_a), (b, out_b))) for tick in range(2)
+        (src.at[tick, pl.ds(n * half, half)], held.at[2 * k + tick, pl.ds(n * half, half)],
+         dst.at[tick, pl.ds(n * half, half)], 4 * k + 2 * tick + n)
+        for k, (src, dst) in enumerate(((a, out_a), (b, out_b))) for tick in range(2) for n in range(2)
     ]
     into = [pltpu.make_async_copy(src, slot, sems.at[0, n]) for src, slot, dst, n in moves]
     back = [pltpu.make_async_copy(slot, dst, sems.at[1, n]) for src, slot, dst, n in moves]
@@ -826,7 +850,6 @@
     ids = jnp.pad(ids, ((0, 0), (0, rows)), constant_values=-1)
 
     any_spec = pl.BlockSpec(memory_space=pl.ANY)
-    vmem_spec = pl.BlockSpec(memory_space=pltpu.VMEM)
 
     def b(*shape):
         return pltpu.VMEM(shape, BF16)
@@ -858,19 +881,20 @@
         f(line, 128), f(line, 128), f(line, 128), f(line, 128),
         f(rows, 128), f(rows, 128), f(rows, 128),
         f(2 * rows, 128), f(2, 2 * rows, 128), f(2, rows, 128),
+        f(1, width), f(1, width), b(8, width), b(8, width), i(8, 2 * rows),
         b(HEAD, line // 2, cw), b(HEAD, line // 2, cw),
         i(2 * rows, 8), i(8, 2 * rows), i(8, 2 * rows), i(8, 2 * rows),
         dma(6), dma(6), dma(2),
         dma(4), dma(4, nc), dma(3), dma(3, nc), dma(3), dma(3, nc),
         dma(2), dma(2, nc), dma(2), dma(2, nc), dma(2), dma(2, nc),
         dma(2, 2), dma(2, 2, nc), dma(2),
-        dma(1), dma(1), dma(1), dma(1), dma(1), dma(1), dma(1), dma(1), dma(2), dma(2), dma(1), dma(HEAD),
+        dma(1), dma(1), dma(1), dma(1), dma(1), dma(1), dma(1), dma(1), dma(2), dma(2), dma(1), dma(HEAD), dma(5),
     ]
     out_shape = jax.ShapeDtypeStruct((2, rows, width), BF16)
     call = pl.pallas_call(
         functools.partial(kernel, (rows, width, cap, hid, sections)),
         out_shape=(out_shape, out_shape),
-        in_specs=[any_spec] * 5 + [vmem_spec] * 4 + [any_spec] * 6 + [vmem_spec],
+        in_specs=[any_spec] * 16,
         out_specs=(any_spec, any_spec),
         scratch_shapes=scratch,
         compiler_params=pltpu.CompilerParams(
@@ -888,7 +912,7 @@
         out_shape=(out_shape, out_shape),
         in_specs=[any_spec] * 2,
         out_specs=(any_spec, any_spec),
-        scratch_shapes=[b(4, rows, width), dma(2, 4)],
+        scratch_shapes=[b(4, rows, width), dma(2, 8)],
     )(out_f, out_b)
     return out_f[None], out_b[None]
 

time: 174 us -> 173 us (level)
  no operation moved by 1% of the time
where the time goes in v3:
time: 173 us
  Pallas kernels  171 us (99%)
    pallas_call x1, Pallas kernels, per_device(): call(act_in[0], grad_in[0], feed[0], loss_grad[0], saved[0], fwd_gain, bw...  168 us

profile of v3, /device:TPU:96, one launch (start us, length us, event | category | flops | bytes accessed | tf_op | source)
XLA Modules:
  0.0 172.8 jit_solution(3560481008208037785)
XLA Ops:
  0.6 0.7 pad_add_fusion
  1.3 0.6 pad.4.refs_15_
  1.9 168.4 %shard_map.176 = (bf16[2,64,3584]{2,1,0:T(8,128)(2,1)}, bf16[2,64,3584]{2,1,0:T(8,128)(2,1)}) custom-call(bf16[64,3584]{1,0:T(8,128)(2,1)} %bitcast.31, bf16[64,3584]{1,0:T(8,128)(2,1)} %bitcast.32, bf16[64,3584]{1,0:T(8,128)(2,1)} %bitcast.33, bf16[64,3584]{1,0:T(8,128)(2,1)} %bitcast.34, bf16[2,64,3584]{2,1,0:T(8,128)(2,1)} %bitcast.30, ...), custom_call_target="tpu_custom_call" | custom-call | tf_op jit(solution)/shard_map/pallas_call | solution.py:904
  170.4 2.4 %shard_map.177 = (bf16[2,64,3584]{2,1,0:T(8,128)(2,1)}, bf16[2,64,3584]{2,1,0:T(8,128)(2,1)}) custom-call(bf16[2,64,3584]{2,1,0:T(8,128)(2,1)} %get-tuple-element.6.a, bf16[2,64,3584]{2,1,0:T(8,128)(2,1)} %get-tuple-element.7.b), custom_call_target="tpu_custom_call" | custom-call | tf_op jit(solution)/shard_map/pallas_call | solution.py:910
